TPU v7x, 32 devices: a whole 2x2x4 slice. The times are simulated.
32 devices in a mesh: gx: 8 (over z, y), gy: 4 (over x, core).
Axes of the slice: x: 2, y: 2, z: 4, core: 2. Of those that a mesh axis runs over, the one named last changes fastest.
Arguments:
- stored_slab: bfloat16 [2, 32, 64, 512], P(None, None, 'gx', 'gy'), may hold values from -6 to 6
- block_scales: bfloat16 [2, 32, 8, 4], P(None, None, 'gx', 'gy'), may hold values from 0.5 to 2
- holder: int32 [4], replicated, may hold values from 0 to 3, each once
- soil_class: int32 [64, 512], P('gx', 'gy'), may hold values from 0 to 11
- soil_table: float32 [12, 4], replicated, may hold values from 0.01 to 0.05
- cotangent: float32 [2, 32, 64, 512], P(None, None, 'gx', 'gy'), may hold values from -6 to 6
Outputs:
- recomputed: float32 [2, 32, 64, 512], P(None, None, 'gx', 'gy')
- sensitivity: float32 [2, 32, 64, 512], P(None, None, 'gx', 'gy')
Inputs may be any that keep to these rules, and one draw needn't show every extreme that they name: holder is a permutation: every gy index holds exactly one checkpoint block.
All inputs are finite; a program needn't handle non-finite values.
Results may differ from a plain program's by a relative error of at most 0.0003.
Values may be sent and summed in bfloat16 or wider, within the bound.
A program may use at most 128 MiB of HBM per device.

v0:
```python
import functools

import jax
import jax.numpy as jnp
from jax import lax
from jax.experimental import pallas as pl
from jax.experimental.pallas import tpu as pltpu
from jax.sharding import PartitionSpec as P

MESH = pl.DeviceIdType.MESH
COT, ST0, ST1, ADJ = range(4)


def window(
    n_gx, n_gy, nz, holder, table, slab, scale, classes, cot, out2, outs,
    slots, sslots, m0, m1, g0, g1, left0, right0, xs, xr, sx, ys, yr, sy, coef,
    gsend, grecv, lsem, xsend, xrecv, ysend, yrecv,
):
    gx, gy = lax.axis_index("gx"), lax.axis_index("gy")
    cx, cy = classes.shape
    half = n_gy // 2
    partner = gy + 1 - 2 * lax.rem(gy, 2)
    lane = lax.broadcasted_iota(jnp.int32, (cx, cy), 1)
    sub = lax.broadcasted_iota(jnp.int32, (cx, cy), 0)
    first_row, last_row = sub == 0, sub == cx - 1
    first_lane, last_lane = lane == 0, lane == cy - 1
    x_has = (gx > 0, gx < n_gx - 1)
    y_has = (gy > 0, gy < n_gy - 1)

    barrier = pltpu.get_barrier_semaphore()
    for k in range(1, n_gy):
        pl.semaphore_signal(barrier, inc=1, device_id=(gx, lax.rem(gy + k, n_gy)), device_id_type=MESH)
    for side, there in ((0, gx - 1), (1, gx + 1)):
        @pl.when(x_has[side])
        def _():
            pl.semaphore_signal(barrier, inc=1, device_id=(there, gy), device_id_type=MESH)

    own = [
        pltpu.make_async_copy(slab, slots.at[gy], lsem.at[0]),
        pltpu.make_async_copy(scale, sslots.at[gy], lsem.at[1]),
    ]
    for copy in own:
        copy.start()

    for side in range(2):
        @pl.when(jnp.logical_not(x_has[side]))
        def _():
            for e in range(4):
                xr[e, side] = jnp.zeros(xr.shape[2:], jnp.float32)

        @pl.when(jnp.logical_not(y_has[side]))
        def _():
            for e in range(3):
                yr[e, side] = jnp.zeros((cx, cy), jnp.float32)

    for ref in (m0, m1, g0, g1):
        for q in range(ref.shape[0]):
            ref[q, 0] = jnp.zeros((cx, cy), jnp.float32)
            ref[q, nz + 1] = jnp.zeros((cx, cy), jnp.float32)

    def to_lane(value, lane_from, lane_to):
        return pltpu.roll(value, lax.rem(lane_to - lane_from + cy, cy), 1)

    def edges_x(e, row, value):
        xs[e, 0, row] = value[0:1]
        xs[e, 1, row] = value[cx - 1 : cx]

    def edges_y(carry, slot, value):
        low, high = carry
        here = lane == slot
        return (
            jnp.where(here, to_lane(value, 0, slot), low),
            jnp.where(here, to_lane(value, cy - 1, slot), high),
        )

    blank = (jnp.zeros((cx, cy), jnp.float32),) * 2

    kind = classes[...]
    for k in range(4):
        value = jnp.zeros((cx, cy), jnp.float32)
        for c in range(table.shape[0]):
            value = jnp.where(kind == c, table[c, k], value)
        coef[0, k] = value
        edges_x(COT, 2 * nz + k, value)

    def cot_layer(z, carry):
        for f in range(2):
            value = cot[f * nz + z]
            g0[f, z + 1] = value
            edges_x(COT, f * nz + z, value)
            carry = edges_y(carry, f * nz + z, value)
        return carry

    carry = lax.fori_loop(0, nz, cot_layer, blank, unroll=4)
    for k in range(4):
        carry = edges_y(carry, 2 * nz + k, coef[0, k])
    ys[0, 0], ys[0, 1] = carry

    def x_copy(e, side):
        there = gx - 1 if side == 0 else gx + 1
        return pltpu.make_async_remote_copy(
            src_ref=xs.at[e, side], dst_ref=xr.at[e, 1 - side],
            send_sem=xsend.at[e, side], recv_sem=xrecv.at[e, 1 - side],
            device_id=(there, gy), device_id_type=MESH,
        )

    def y_copy(e, side):
        there = gy - 1 if side == 0 else gy + 1
        return pltpu.make_async_remote_copy(
            src_ref=ys.at[e, side], dst_ref=yr.at[e, 1 - side],
            send_sem=ysend.at[e, side], recv_sem=yrecv.at[e, 1 - side],
            device_id=(gx, there), device_id_type=MESH,
        )

    def for_sides(make, has, e, act):
        for side in range(2):
            @pl.when(has[side])
            def _():
                act(make(e, side))

    def start(c):
        c.start()

    def arrived(make, has, e):
        for side in range(2):
            @pl.when(has[side])
            def _():
                make(e, 1 - side).wait_recv()

    def block_copies(index, slot, there, mine):
        src, ssrc = (slab, scale) if mine else (slots.at[slot], sslots.at[slot])
        return [
            pltpu.make_async_remote_copy(
                src_ref=a, dst_ref=b.at[slot], send_sem=gsend.at[i, index],
                recv_sem=grecv.at[i, index], device_id=(gx, there), device_id_type=MESH,
            )
            for i, (a, b) in enumerate(((src, slots), (ssrc, sslots)))
        ]

    greeted = n_gy - 1 + jnp.where(gx > 0, 1, 0) + jnp.where(gx < n_gx - 1, 1, 0)
    pl.semaphore_wait(barrier, greeted)

    sent = []
    for k in range(1, half):
        sent += block_copies(k, gy, lax.rem(gy + 2 * k, n_gy), True)
    sent += block_copies(0, gy, partner, True)
    for c in sent:
        c.start()
    for_sides(y_copy, y_has, 0, start)
    for_sides(x_copy, x_has, COT, start)
    for k in range(1, half):
        for c in sent[2 * k - 2 : 2 * k]:
            c.wait_recv()
        onward = block_copies(half - 1 + k, lax.rem(gy - 2 * k + n_gy, n_gy), partner, False)
        for c in onward:
            c.start()
        sent += onward
    for c in sent[2 * half - 2 :]:
        c.wait_recv()
    for copy in own:
        copy.wait()

    def block_layers(index, factor, put):
        here = holder[index]
        factors = sslots[here] * factor

        def pair(p, _):
            both = slots[here, p].astype(jnp.float32)
            for j in range(2):
                l = 2 * p + j
                by = jnp.broadcast_to(to_lane(factors, l, 0)[:, 0:1], (cx, cy))
                put(l, both[j * cx : (j + 1) * cx] * by)
            return 0

        return pair

    def strength(u):
        return 1.5 + jnp.tanh(u)

    def put_own(l, value):
        f, z = l // nz, lax.rem(l, nz)
        m0[f, z + 1] = value
        edges_x(ST0, l, value)

    lax.fori_loop(0, nz, block_layers(gy, 1.0, put_own), 0, unroll=2)
    for_sides(x_copy, x_has, ST0, start)

    def put_near(ref):
        def put(l, value):
            ref[l // nz, lax.rem(l, nz)] = value
        return put

    before = block_layers(jnp.maximum(gy - 1, 0), jnp.where(gy > 0, 1.0, 0.0), put_near(left0))
    after = block_layers(jnp.minimum(gy + 1, n_gy - 1), jnp.where(gy < n_gy - 1, 1.0, 0.0), put_near(right0))

    def sides_of(p, _):
        before(p, 0)
        after(p, 0)
        return 0

    lax.fori_loop(0, nz, sides_of, 0, unroll=2)

    def strengths0(z, _):
        s = strength(m0[0, z + 1])
        m0[2, z + 1] = s
        m0[3, z + 1] = 0.75 + 0.5 * s
        left0[2, z] = strength(left0[0, z])
        right0[2, z] = strength(right0[0, z])
        return 0

    lax.fori_loop(0, nz, strengths0, 0, unroll=4)

    arrived(y_copy, y_has, 0)
    arrived(x_copy, x_has, COT)

    def beside_x(value, low, high):
        return (
            jnp.where(first_row, low, pltpu.roll(value, 1, 0)),
            jnp.where(last_row, high, pltpu.roll(value, cx - 1, 0)),
        )

    def beside_y(value, low, high, slot):
        return (
            jnp.where(first_lane, to_lane(low, slot, 0), pltpu.roll(value, 1, 1)),
            jnp.where(last_lane, to_lane(high, slot, cy - 1), pltpu.roll(value, cy - 1, 1)),
        )

    for k in range(4):
        value = coef[0, k]
        row = 2 * nz + k
        near = beside_x(value, xr[COT, 0, row], xr[COT, 1, row]) + beside_y(
            value, yr[0, 0], yr[0, 1], row
        )
        for d in range(4):
            coef[1 + d, k] = near[d]

    def near_strengths(e, side_count=2):
        for side in range(2):
            def layer(z, _):
                sx[side, z] = strength(xr[e, side, z])
                return 0
            lax.fori_loop(0, nz, layer, 0, unroll=8)

    def rows(e, row):
        return xr[e, 0, row], xr[e, 1, row]

    def state_near(level, z):
        m = m0 if level == 0 else m1
        e = ST0 if level == 0 else ST1
        found = []
        for q in range(3):
            value = m[q, z + 1]
            if q < 2:
                low, high = rows(e, q * nz + z)
            else:
                low, high = sx[0, z], sx[1, z]
            near = beside_x(value, low, high)
            if level == 0:
                near += (
                    pltpu.roll(jnp.where(last_lane, left0[q, z], value), 1, 1),
                    pltpu.roll(jnp.where(first_lane, right0[q, z], value), cy - 1, 1),
                )
            elif q < 2:
                near += beside_y(value, yr[1, 0], yr[1, 1], q * nz + z)
            else:
                near += beside_y(value, sy[0], sy[1], z)
            found.append((value,) + near)
        return found

    def forward(level, z):
        m = m0 if level == 0 else m1
        us, ts, ss = state_near(level, z)
        u, t, s = us[0], ts[0], ss[0]
        h = m[3, z + 1]
        c0, c1, c2, c3 = (coef[0, k] for k in range(4))
        kw, dtv, lamb, kv = c0 * s, c1 * h, c2 * h, c3 * s
        a = b = None
        for zn in (z, z + 2):
            x = (s + m[2, zn]) * (m[0, zn] - u)
            y = (h + m[3, zn]) * (m[1, zn] - t)
            a, b = (x, y) if a is None else (a + x, b + y)
        water, energy = c0 * a + c1 * b, c2 * b + c3 * a
        for d in range(1, 5):
            sn = ss[d]
            hn = 0.75 + 0.5 * sn
            du, dt = us[d] - u, ts[d] - t
            water += (kw + coef[d, 0] * sn) * du + (dtv + coef[d, 1] * hn) * dt
            energy += (lamb + coef[d, 2] * hn) * dt + (kv + coef[d, 3] * sn) * du
        return u + 0.5 * water, t + 0.5 * energy

    def backward(level, z):
        m, g, ge, gy_slot = (m0, g1, ADJ, 2) if level == 0 else (m1, g0, COT, 0)
        us, ts, ss = state_near(level, z)
        u, t, s = us[0], ts[0], ss[0]
        h = m[3, z + 1]
        c0, c1, c2, c3 = (coef[0, k] for k in range(4))
        kw, dtv, lamb, kv = c0 * s, c1 * h, c2 * h, c3 * s
        gws, ges = [], []
        for q, into in ((0, gws), (1, ges)):
            value = g[q, z + 1]
            into.append(value)
            into += beside_x(value, *rows(ge, q * nz + z))
            into += beside_y(value, yr[gy_slot, 0], yr[gy_slot, 1], q * nz + z)
        w, e = gws[0], ges[0]
        pu = pt = q1 = q2 = q3 = q4 = 0.0
        for zn in (z, z + 2):
            du, dt = m[0, zn] - u, m[1, zn] - t
            dw, de = g[0, zn] - w, g[1, zn] - e
            sp, hp = s + m[2, zn], h + m[3, zn]
            pu += sp * (c0 * dw + c3 * de)
            pt += hp * (c1 * dw + c2 * de)
            q1, q2, q3, q4 = q1 + du * dw, q2 + du * de, q3 + dt * dw, q4 + dt * de
        for d in range(1, 5):
            sn = ss[d]
            hn = 0.75 + 0.5 * sn
            du, dt = us[d] - u, ts[d] - t
            dw, de = gws[d] - w, ges[d] - e
            pu += (kw + coef[d, 0] * sn) * dw + (kv + coef[d, 3] * sn) * de
            pt += (dtv + coef[d, 1] * hn) * dw + (lamb + coef[d, 2] * hn) * de
            q1, q2, q3, q4 = q1 + du * dw, q2 + du * de, q3 + dt * dw, q4 + dt * de
        bend = s - 1.5
        slope = 1.0 - bend * bend
        pu -= slope * (c0 * q1 + c3 * q2 + 0.5 * (c1 * q3 + c2 * q4))
        return w + 0.5 * pu, e + 0.5 * pt

    arrived(x_copy, x_has, ST0)
    near_strengths(ST0)

    def step1(z, carry):
        pair = forward(0, z)
        for f in range(2):
            m1[f, z + 1] = pair[f]
            edges_x(ST1, f * nz + z, pair[f])
            carry = edges_y(carry, f * nz + z, pair[f])
        s = strength(pair[0])
        m1[2, z + 1] = s
        m1[3, z + 1] = 0.75 + 0.5 * s
        return carry

    ys[1, 0], ys[1, 1] = lax.fori_loop(0, nz, step1, blank, unroll=2)
    for_sides(x_copy, x_has, ST1, start)
    for_sides(y_copy, y_has, 1, start)
    arrived(x_copy, x_has, ST1)
    arrived(y_copy, y_has, 1)
    near_strengths(ST1)
    for side in range(2):
        sy[side] = strength(yr[1, side])

    def step2(z, carry):
        pair = backward(1, z)
        for f in range(2):
            g1[f, z + 1] = pair[f]
            edges_x(ADJ, f * nz + z, pair[f])
            carry = edges_y(carry, f * nz + z, pair[f])
        return carry

    ys[2, 0], ys[2, 1] = lax.fori_loop(0, nz, step2, blank, unroll=2)
    for_sides(x_copy, x_has, ADJ, start)
    for_sides(y_copy, y_has, 2, start)

    def step3(z, _):
        pair = forward(1, z)
        for f in range(2):
            out2[f * nz + z] = pair[f]
        return 0

    lax.fori_loop(0, nz, step3, 0, unroll=2)
    arrived(x_copy, x_has, ADJ)
    arrived(y_copy, y_has, 2)
    near_strengths(ST0)

    def step4(z, _):
        pair = backward(0, z)
        for f in range(2):
            outs[f * nz + z] = pair[f]
        return 0

    lax.fori_loop(0, nz, step4, 0, unroll=2)

    for c in sent:
        c.wait_send()
    for e in range(4):
        for_sides(x_copy, x_has, e, lambda c: c.wait_send())
    for e in range(3):
        for_sides(y_copy, y_has, e, lambda c: c.wait_send())


def on_device(n_gx, n_gy, stored_slab, block_scales, holder, soil_class, soil_table, cotangent):
    _, nz, cx, cy = stored_slab.shape
    layers = 2 * nz
    assert n_gy % 2 == 0 and layers + 4 <= cy
    f32 = jnp.float32
    slab = stored_slab.reshape(nz, 2 * cx, cy)
    factors = jnp.zeros((cy,), f32).at[:layers].set(block_scales.reshape(layers).astype(f32))
    factors = jnp.broadcast_to(factors[None], (cx, cy))
    cot = cotangent.reshape(layers, cx, cy)
    vmem = pl.BlockSpec(memory_space=pltpu.VMEM)
    smem = pl.BlockSpec(memory_space=pltpu.SMEM)
    out = jax.ShapeDtypeStruct((layers, cx, cy), f32)
    dma = pltpu.SemaphoreType.DMA
    state2, adjoint0 = pl.pallas_call(
        functools.partial(window, n_gx, n_gy, nz),
        out_shape=(out, out),
        in_specs=[smem, smem, vmem, vmem, vmem, vmem],
        out_specs=(vmem, vmem),
        scratch_shapes=[
            pltpu.VMEM((n_gy, nz, 2 * cx, cy), jnp.bfloat16),
            pltpu.VMEM((n_gy, cx, cy), f32),
            pltpu.VMEM((4, nz + 2, cx, cy), f32),
            pltpu.VMEM((4, nz + 2, cx, cy), f32),
            pltpu.VMEM((2, nz + 2, cx, cy), f32),
            pltpu.VMEM((2, nz + 2, cx, cy), f32),
            pltpu.VMEM((3, nz, cx, cy), f32),
            pltpu.VMEM((3, nz, cx, cy), f32),
            pltpu.VMEM((4, 2, layers + 4, 1, cy), f32),
            pltpu.VMEM((4, 2, layers + 4, 1, cy), f32),
            pltpu.VMEM((2, nz, 1, cy), f32),
            pltpu.VMEM((3, 2, cx, cy), f32),
            pltpu.VMEM((3, 2, cx, cy), f32),
            pltpu.VMEM((2, cx, cy), f32),
            pltpu.VMEM((5, 4, cx, cy), f32),
            dma((2, n_gy - 1)),
            dma((2, n_gy - 1)),
            dma((2,)),
            dma((4, 2)),
            dma((4, 2)),
            dma((3, 2)),
            dma((3, 2)),
        ],
        compiler_params=pltpu.CompilerParams(
            collective_id=0, has_side_effects=True, vmem_limit_bytes=32 * 1024 * 1024
        ),
        name="window",
    )(holder, soil_table, slab, factors, soil_class, cot)
    shape = cotangent.shape
    return state2.reshape(shape), adjoint0.reshape(shape)


def solution(mesh):
    placed = (
        P(None, None, "gx", "gy"),
        P(None, None, "gx", "gy"),
        P(),
        P("gx", "gy"),
        P(),
        P(None, None, "gx", "gy"),
    )
    return jax.shard_map(
        functools.partial(on_device, mesh.shape["gx"], mesh.shape["gy"]),
        mesh=mesh,
        in_specs=placed,
        out_specs=(P(None, None, "gx", "gy"), P(None, None, "gx", "gy")),
        check_vma=False,
    )
```

profile of v0, /device:TPU:0, one launch (start us, length us, event | category | flops | bytes accessed | tf_op | source)
XLA Modules:
  0.0 35.9 jit_solution(10089018724995762353)
XLA Ops:
  0.6 0.0 copy-start.5
  0.6 0.6 %copy-done.5 = bf16[2,32,1,1]{1,0,3,2:T(2,128)(2,1)S(1)} copy-done((bf16[2,32,1,1]{1,0,3,2:T(2,128)(2,1)S(1)}, bf16[2,32,1,1]{1,0,3,2:T(2,128)(2,1)}, u32[]{:S(2)}) %copy-start.5) | copy-done | bytes 152
  1.3 0.1 convert_element_type.5
  1.4 0.0 copy-start.4
  1.4 0.7 %copy-done.4 = f32[12,4]{0,1:T(4,128)S(1)} copy-done((f32[12,4]{0,1:T(4,128)S(1)}, f32[12,4]{0,1:T(4,128)}, u32[]{:S(2)}) %copy-start.4) | copy-done | bytes 216
  2.1 0.0 copy-start.2
  2.1 0.0 copy-start.3
  2.1 0.1 copy.8.table
  2.2 0.6 %copy-done.2 = s32[8,128]{1,0:T(8,128)S(1)} copy-done((s32[8,128]{1,0:T(8,128)S(1)}, s32[8,128]{1,0:T(8,128)}, u32[]{:S(2)}) %copy-start.2) | copy-done | bytes 4120
  2.7 0.0 copy-done.3
  2.7 0.0 copy-start
  2.8 0.9 %copy-done = f32[2,32,8,128]{3,2,1,0:T(8,128)S(1)} copy-done((f32[2,32,8,128]{3,2,1,0:T(8,128)S(1)}, f32[2,32,8,128]{3,2,1,0:T(8,128)}, u32[]{:S(2)}) %copy-start) | copy-done | bytes 262168
  3.7 0.0 copy-start.1
  3.7 0.9 %copy-done.1 = bf16[2,32,8,128]{3,2,1,0:T(8,128)(2,1)S(1)} copy-done((bf16[2,32,8,128]{3,2,1,0:T(8,128)(2,1)S(1)}, bf16[2,32,8,128]{3,2,1,0:T(8,128)(2,1)}, u32[]{:S(2)}) %copy-start.1) | copy-done | bytes 131096
  4.6 29.9 %window.1 = (f32[64,8,128]{2,1,0:T(8,128)S(1)}, f32[64,8,128]{2,1,0:T(8,128)S(1)}) custom-call(s32[4]{0:T(128)S(1)} %copy-done.3, f32[12,4]{1,0:T(8,128)S(1)} %copy.8.table, bf16[32,16,128]{2,1,0:T(8,128)(2,1)S(1)} %bitcast.9, f32[8,128]{1,0:T(8,128)S(1)} %broadcast_in_dim.2.scale, s32[8,128]{1,0:T(8,128)S(1)} %copy-done.2, f32[64,8,128]{2,1,0:T(8,128)S(1)} %bitcast.6), custom_call_target="tpu_custom_call" | custom-call | tf_op jit(solution)/shard_map/window/pallas_call | solution.py:401
  34.5 0.7 %copy.11 = f32[2,32,8,128]{3,2,1,0:T(8,128)} copy(f32[2,32,8,128]{3,2,1,0:T(8,128)S(1)} %bitcast.8) | data formatting | bytes 524288
  35.2 0.7 %copy.12 = f32[2,32,8,128]{3,2,1,0:T(8,128)} copy(f32[2,32,8,128]{3,2,1,0:T(8,128)S(1)} %bitcast.7) | data formatting | bytes 524288
  (2 shorter events, 0.0 us)
Async XLA Ops:
  0.6 0.7 %copy-start.5 = (bf16[2,32,1,1]{1,0,3,2:T(2,128)(2,1)S(1)}, bf16[2,32,1,1]{1,0,3,2:T(2,128)(2,1)}, u32[]{:S(2)}) copy-start(bf16[2,32,1,1]{1,0,3,2:T(2,128)(2,1)} %param.9) | copy-start | bytes 388
  1.4 0.7 %copy-start.4 = (f32[12,4]{0,1:T(4,128)S(1)}, f32[12,4]{0,1:T(4,128)}, u32[]{:S(2)}) copy-start(f32[12,4]{0,1:T(4,128)} %param.12) | copy-start | bytes 580
  2.1 0.7 %copy-start.2 = (s32[8,128]{1,0:T(8,128)S(1)}, s32[8,128]{1,0:T(8,128)}, u32[]{:S(2)}) copy-start(s32[8,128]{1,0:T(8,128)} %classes.1) | copy-start | bytes 12292
  2.1 0.7 %copy-start.3 = (s32[4]{0:T(128)S(1)}, s32[4]{0:T(128)}, u32[]{:S(2)}) copy-start(s32[4]{0:T(128)} %holder.1) | copy-start | bytes 52
  2.7 1.0 %copy-start = (f32[2,32,8,128]{3,2,1,0:T(8,128)S(1)}, f32[2,32,8,128]{3,2,1,0:T(8,128)}, u32[]{:S(2)}) copy-start(f32[2,32,8,128]{3,2,1,0:T(8,128)} %param.13) | copy-start | bytes 786436
  3.7 0.9 %copy-start.1 = (bf16[2,32,8,128]{3,2,1,0:T(8,128)(2,1)S(1)}, bf16[2,32,8,128]{3,2,1,0:T(8,128)(2,1)}, u32[]{:S(2)}) copy-start(bf16[2,32,8,128]{3,2,1,0:T(8,128)(2,1)} %param.8) | copy-start | bytes 393220
where the time goes:
time: 36.1 us; the launch traced here: 35.9 us
  Pallas kernels  29.9 us (83%)
  local copies, waits for them, and re-layouts  5.36 us (15%)
  between operations  0.65 us (2%)
    pallas_call x1, Pallas kernels, on_device(): pl.pallas_call(functools.partial(window, n_gx, n_gy, nz), out_shape=(out,...  29.9 us
    unnamed x15, local copies, waits for them, and re-layouts  5.27 us

commit v1 on v0

v1 whole, which is shorter than its diff:
```python
import functools

import jax
import jax.numpy as jnp
from jax import lax
from jax.experimental import pallas as pl
from jax.experimental.pallas import tpu as pltpu
from jax.sharding import PartitionSpec as P

MESH = pl.DeviceIdType.MESH
COT, ST0, ST1, ADJ = range(4)


def window(
    n_gx, n_gy, nz, holder_in, table_in, slab_in, scale, classes_in, cot, out2, outs,
    holder, table, classes, slots, sslots, m0, m1, g0, g1, left0, right0, near0, near1,
    xs, xr, ys, yr, coef, gsend, grecv, lsem, xsend, xrecv, ysend, yrecv,
):
    gx, gy = lax.axis_index("gx"), lax.axis_index("gy")
    cx, cy = classes.shape
    half = n_gy // 2
    partner = gy + 1 - 2 * lax.rem(gy, 2)
    lane = lax.broadcasted_iota(jnp.int32, (cx, cy), 1)
    sub = lax.broadcasted_iota(jnp.int32, (cx, cy), 0)
    first_row, last_row = sub == 0, sub == cx - 1
    first_lane, last_lane = lane == 0, lane == cy - 1
    x_has = (gx > 0, gx < n_gx - 1)
    y_has = (gy > 0, gy < n_gy - 1)

    barrier = pltpu.get_barrier_semaphore()
    for k in range(1, n_gy):
        pl.semaphore_signal(barrier, inc=1, device_id=(gx, lax.rem(gy + k, n_gy)), device_id_type=MESH)
    for side, there in ((0, gx - 1), (1, gx + 1)):
        @pl.when(x_has[side])
        def _():
            pl.semaphore_signal(barrier, inc=1, device_id=(there, gy), device_id_type=MESH)

    small = [
        pltpu.make_async_copy(table_in, table, lsem.at[0]),
        pltpu.make_async_copy(classes_in, classes, lsem.at[1]),
        pltpu.make_async_copy(holder_in, holder, lsem.at[2]),
    ]
    own = [
        pltpu.make_async_copy(slab_in, slots.at[gy], lsem.at[3]),
        pltpu.make_async_copy(scale, sslots.at[gy], lsem.at[4]),
    ]
    cots = [
        pltpu.make_async_copy(
            cot.at[pl.ds(f * nz, nz)], g0.at[f, pl.ds(1, nz)], lsem.at[5 + f]
        )
        for f in range(2)
    ]
    for copy in small + own + cots:
        copy.start()

    for side in range(2):
        @pl.when(jnp.logical_not(x_has[side]))
        def _():
            for e in range(4):
                xr[e, side] = jnp.zeros(xr.shape[2:], jnp.float32)

        @pl.when(jnp.logical_not(y_has[side]))
        def _():
            for e in range(3):
                yr[e, side] = jnp.zeros((cx, cy), jnp.float32)

    for ref in (m0, m1, g0, g1):
        for q in range(ref.shape[0]):
            ref[q, 0] = jnp.zeros((cx, cy), jnp.float32)
            ref[q, nz + 1] = jnp.zeros((cx, cy), jnp.float32)

    def to_lane(value, lane_from, lane_to):
        return pltpu.roll(value, lax.rem(lane_to - lane_from + cy, cy), 1)

    def edges_x(e, row, value):
        xs[e, 0, row] = value[0:1]
        xs[e, 1, row] = value[cx - 1 : cx]

    def edges_y(carry, slot, value):
        low, high = carry
        here = lane == slot
        return (
            jnp.where(here, to_lane(value, 0, slot), low),
            jnp.where(here, to_lane(value, cy - 1, slot), high),
        )

    blank = (jnp.zeros((cx, cy), jnp.float32),) * 2

    def by_chunks(layers, size, work, store, carry):
        def chunk(i, carry):
            zs = [i * size + j for j in range(size)]
            found = [work(z) for z in zs]
            for z, value in zip(zs, found):
                carry = store(z, value, carry)
            return carry

        assert layers % size == 0
        return lax.fori_loop(0, layers // size, chunk, carry)

    for copy in small:
        copy.wait()
    kind = classes[...]
    for k in range(4):
        value = jnp.zeros((cx, cy), jnp.float32)
        for c in range(table.shape[1]):
            value = jnp.where(kind == c, table[k, c], value)
        coef[0, k] = value
        edges_x(COT, 2 * nz + k, value)

    def put_cot(z, values, carry):
        for f in range(2):
            edges_x(COT, f * nz + z, values[f])
            carry = edges_y(carry, f * nz + z, values[f])
        return carry

    for copy in cots:
        copy.wait()
    carry = by_chunks(nz, 8, lambda z: [g0[f, z + 1] for f in range(2)], put_cot, blank)
    for k in range(4):
        carry = edges_y(carry, 2 * nz + k, coef[0, k])
    ys[0, 0], ys[0, 1] = carry

    def x_copy(e, side):
        there = gx - 1 if side == 0 else gx + 1
        return pltpu.make_async_remote_copy(
            src_ref=xs.at[e, side], dst_ref=xr.at[e, 1 - side],
            send_sem=xsend.at[e, side], recv_sem=xrecv.at[e, 1 - side],
            device_id=(there, gy), device_id_type=MESH,
        )

    def y_copy(e, side):
        there = gy - 1 if side == 0 else gy + 1
        return pltpu.make_async_remote_copy(
            src_ref=ys.at[e, side], dst_ref=yr.at[e, 1 - side],
            send_sem=ysend.at[e, side], recv_sem=yrecv.at[e, 1 - side],
            device_id=(gx, there), device_id_type=MESH,
        )

    def for_sides(make, has, e, act):
        for side in range(2):
            @pl.when(has[side])
            def _():
                act(make(e, side))

    def start(c):
        c.start()

    def arrived(make, has, e):
        for side in range(2):
            @pl.when(has[side])
            def _():
                make(e, 1 - side).wait_recv()

    def block_copies(index, slot, there):
        src, ssrc = slots.at[slot], sslots.at[slot]
        return [
            pltpu.make_async_remote_copy(
                src_ref=a, dst_ref=b.at[slot], send_sem=gsend.at[i, index],
                recv_sem=grecv.at[i, index], device_id=(gx, there), device_id_type=MESH,
            )
            for i, (a, b) in enumerate(((src, slots), (ssrc, sslots)))
        ]

    greeted = n_gy - 1 + jnp.where(gx > 0, 1, 0) + jnp.where(gx < n_gx - 1, 1, 0)
    for copy in own:
        copy.wait()
    pl.semaphore_wait(barrier, greeted)

    sent = []
    for k in range(1, half):
        sent += block_copies(k, gy, lax.rem(gy + 2 * k, n_gy))
    sent += block_copies(0, gy, partner)
    for c in sent:
        c.start()
    for_sides(y_copy, y_has, 0, start)
    for_sides(x_copy, x_has, COT, start)
    for k in range(1, half):
        for c in sent[2 * k - 2 : 2 * k]:
            c.wait_recv()
        onward = block_copies(half - 1 + k, lax.rem(gy - 2 * k + n_gy, n_gy), partner)
        for c in onward:
            c.start()
        sent += onward
    for c in sent[2 * half - 2 :]:
        c.wait_recv()

    def strength(u):
        return 1.5 + jnp.tanh(u)

    def pair_of(index, factor):
        here = holder[index]
        factors = sslots[here] * factor

        def pair(p):
            both = slots[here, p].astype(jnp.float32)
            found = []
            for j in range(2):
                by = jnp.broadcast_to(to_lane(factors, 2 * p + j, 0)[:, 0:1], (cx, cy))
                found.append(both[j * cx : (j + 1) * cx] * by)
            return found

        return pair

    def put_own(p, values, _):
        for j in range(2):
            l = 2 * p + j
            m0[l // nz, lax.rem(l, nz) + 1] = values[j]
            edges_x(ST0, l, values[j])
        return 0

    by_chunks(nz, 8, pair_of(gy, 1.0), put_own, 0)
    for_sides(x_copy, x_has, ST0, start)

    before = pair_of(jnp.maximum(gy - 1, 0), jnp.where(gy > 0, 1.0, 0.0))
    after = pair_of(jnp.minimum(gy + 1, n_gy - 1), jnp.where(gy < n_gy - 1, 1.0, 0.0))

    def put_sides(p, values, _):
        for ref, pair in zip((left0, right0), values):
            for j in range(2):
                l = 2 * p + j
                ref[l // nz, lax.rem(l, nz)] = pair[j]
        return 0

    by_chunks(nz, 4, lambda p: (before(p), after(p)), put_sides, 0)

    def put_strength(z, s, _):
        m0[2, z + 1] = s
        m0[3, z + 1] = 0.75 + 0.5 * s
        return 0

    by_chunks(nz, 8, lambda z: strength(m0[0, z + 1]), put_strength, 0)

    arrived(y_copy, y_has, 0)
    arrived(x_copy, x_has, COT)

    def beside_x(value, low, high):
        return (
            jnp.where(first_row, low, pltpu.roll(value, 1, 0)),
            jnp.where(last_row, high, pltpu.roll(value, cx - 1, 0)),
        )

    def beside_y(value, low, high, slot):
        return (
            jnp.where(first_lane, to_lane(low, slot, 0), pltpu.roll(value, 1, 1)),
            jnp.where(last_lane, to_lane(high, slot, cy - 1), pltpu.roll(value, cy - 1, 1)),
        )

    for k in range(4):
        value = coef[0, k]
        row = 2 * nz + k
        near = beside_x(value, xr[COT, 0, row], xr[COT, 1, row]) + beside_y(
            value, yr[0, 0], yr[0, 1], row
        )
        for d in range(4):
            coef[1 + d, k] = near[d]

    def rows(e, row):
        return xr[e, 0, row], xr[e, 1, row]

    def state_near(level, z):
        m, e = (m0, ST0) if level == 0 else (m1, ST1)
        found = []
        for q in range(2):
            value = m[q, z + 1]
            near = beside_x(value, *rows(e, q * nz + z))
            if level == 0:
                near += (
                    pltpu.roll(jnp.where(last_lane, left0[q, z], value), 1, 1),
                    pltpu.roll(jnp.where(first_lane, right0[q, z], value), cy - 1, 1),
                )
            else:
                near += beside_y(value, yr[1, 0], yr[1, 1], q * nz + z)
            found.append(near)
        found.append([strength(u) for u in found[0]])
        return found

    def keep_near(ref, z, found):
        for q in range(3):
            for d in range(4):
                ref[4 * q + d, z] = found[q][d]

    def kept_near(ref, z):
        return [[ref[4 * q + d, z] for d in range(4)] for q in range(3)]

    def forward(level, z, near):
        m = m0 if level == 0 else m1
        us, ts, ss = near
        u, t, s, h = (m[q, z + 1] for q in range(4))
        c0, c1, c2, c3 = (coef[0, k] for k in range(4))
        kw, dtv, lamb, kv = c0 * s, c1 * h, c2 * h, c3 * s
        a = b = None
        for zn in (z, z + 2):
            x = (s + m[2, zn]) * (m[0, zn] - u)
            y = (h + m[3, zn]) * (m[1, zn] - t)
            a, b = (x, y) if a is None else (a + x, b + y)
        water, energy = c0 * a + c1 * b, c2 * b + c3 * a
        for d in range(4):
            sn = ss[d]
            hn = 0.75 + 0.5 * sn
            du, dt = us[d] - u, ts[d] - t
            water += (kw + coef[1 + d, 0] * sn) * du + (dtv + coef[1 + d, 1] * hn) * dt
            energy += (lamb + coef[1 + d, 2] * hn) * dt + (kv + coef[1 + d, 3] * sn) * du
        return u + 0.5 * water, t + 0.5 * energy

    def backward(level, z, near):
        m, g, ge, gy_slot = (m0, g1, ADJ, 2) if level == 0 else (m1, g0, COT, 0)
        us, ts, ss = near
        u, t, s, h = (m[q, z + 1] for q in range(4))
        c0, c1, c2, c3 = (coef[0, k] for k in range(4))
        kw, dtv, lamb, kv = c0 * s, c1 * h, c2 * h, c3 * s
        gws, ges = [], []
        for q, into in ((0, gws), (1, ges)):
            value = g[q, z + 1]
            into.append(value)
            into += beside_x(value, *rows(ge, q * nz + z))
            into += beside_y(value, yr[gy_slot, 0], yr[gy_slot, 1], q * nz + z)
        w, e = gws[0], ges[0]
        pu = pt = q1 = q2 = q3 = q4 = 0.0
        for zn in (z, z + 2):
            du, dt = m[0, zn] - u, m[1, zn] - t
            dw, de = g[0, zn] - w, g[1, zn] - e
            sp, hp = s + m[2, zn], h + m[3, zn]
            pu += sp * (c0 * dw + c3 * de)
            pt += hp * (c1 * dw + c2 * de)
            q1, q2, q3, q4 = q1 + du * dw, q2 + du * de, q3 + dt * dw, q4 + dt * de
        for d in range(4):
            sn = ss[d]
            hn = 0.75 + 0.5 * sn
            du, dt = us[d] - u, ts[d] - t
            dw, de = gws[1 + d] - w, ges[1 + d] - e
            pu += (kw + coef[1 + d, 0] * sn) * dw + (kv + coef[1 + d, 3] * sn) * de
            pt += (dtv + coef[1 + d, 1] * hn) * dw + (lamb + coef[1 + d, 2] * hn) * de
            q1, q2, q3, q4 = q1 + du * dw, q2 + du * de, q3 + dt * dw, q4 + dt * de
        bend = s - 1.5
        slope = 1.0 - bend * bend
        pu -= slope * (c0 * q1 + c3 * q2 + 0.5 * (c1 * q3 + c2 * q4))
        return w + 0.5 * pu, e + 0.5 * pt

    def put_edges(e, ref, z, pair, carry):
        for f in range(2):
            ref[f, z + 1] = pair[f]
            edges_x(e, f * nz + z, pair[f])
            carry = edges_y(carry, f * nz + z, pair[f])
        return carry

    arrived(x_copy, x_has, ST0)

    def work1(z):
        near = state_near(0, z)
        pair = forward(0, z, near)
        return near, pair, strength(pair[0])

    def put1(z, found, carry):
        near, pair, s = found
        keep_near(near0, z, near)
        m1[2, z + 1] = s
        m1[3, z + 1] = 0.75 + 0.5 * s
        return put_edges(ST1, m1, z, pair, carry)

    ys[1, 0], ys[1, 1] = by_chunks(nz, 4, work1, put1, blank)
    for_sides(x_copy, x_has, ST1, start)
    for_sides(y_copy, y_has, 1, start)
    arrived(x_copy, x_has, ST1)
    arrived(y_copy, y_has, 1)

    def work2(z):
        near = state_near(1, z)
        return near, backward(1, z, near)

    def put2(z, found, carry):
        near, pair = found
        keep_near(near1, z, near)
        return put_edges(ADJ, g1, z, pair, carry)

    ys[2, 0], ys[2, 1] = by_chunks(nz, 4, work2, put2, blank)
    for_sides(x_copy, x_has, ADJ, start)
    for_sides(y_copy, y_has, 2, start)

    def put_out(ref):
        def put(z, pair, _):
            for f in range(2):
                ref[f * nz + z] = pair[f]
            return 0
        return put

    by_chunks(nz, 4, lambda z: forward(1, z, kept_near(near1, z)), put_out(out2), 0)
    arrived(x_copy, x_has, ADJ)
    arrived(y_copy, y_has, 2)
    by_chunks(nz, 4, lambda z: backward(0, z, kept_near(near0, z)), put_out(outs), 0)

    for c in sent:
        c.wait_send()
    for e in range(4):
        for_sides(x_copy, x_has, e, lambda c: c.wait_send())
    for e in range(3):
        for_sides(y_copy, y_has, e, lambda c: c.wait_send())


def on_device(n_gx, n_gy, stored_slab, block_scales, holder, soil_class, soil_table, cotangent):
    _, nz, cx, cy = stored_slab.shape
    layers = 2 * nz
    assert n_gy % 2 == 0 and layers + 4 <= cy
    f32 = jnp.float32
    slab = stored_slab.reshape(nz, 2 * cx, cy)
    factors = jnp.zeros((cy,), f32).at[:layers].set(block_scales.reshape(layers).astype(f32))
    factors = jnp.broadcast_to(factors[None], (cx, cy))
    cot = cotangent.reshape(layers, cx, cy)
    vmem = pl.BlockSpec(memory_space=pltpu.VMEM)
    hbm = pl.BlockSpec(memory_space=pltpu.HBM)
    out = jax.ShapeDtypeStruct((layers, cx, cy), f32)
    dma = pltpu.SemaphoreType.DMA
    state2, adjoint0 = pl.pallas_call(
        functools.partial(window, n_gx, n_gy, nz),
        out_shape=(out, out),
        in_specs=[hbm, hbm, hbm, vmem, hbm, hbm],
        out_specs=(vmem, vmem),
        scratch_shapes=[
            pltpu.SMEM(holder.shape, jnp.int32),
            pltpu.SMEM(soil_table.shape[::-1], f32),
            pltpu.VMEM((cx, cy), jnp.int32),
            pltpu.VMEM((n_gy, nz, 2 * cx, cy), jnp.bfloat16),
            pltpu.VMEM((n_gy, cx, cy), f32),
            pltpu.VMEM((4, nz + 2, cx, cy), f32),
            pltpu.VMEM((4, nz + 2, cx, cy), f32),
            pltpu.VMEM((2, nz + 2, cx, cy), f32),
            pltpu.VMEM((2, nz + 2, cx, cy), f32),
            pltpu.VMEM((2, nz, cx, cy), f32),
            pltpu.VMEM((2, nz, cx, cy), f32),
            pltpu.VMEM((12, nz, cx, cy), f32),
            pltpu.VMEM((12, nz, cx, cy), f32),
            pltpu.VMEM((4, 2, layers + 4, 1, cy), f32),
            pltpu.VMEM((4, 2, layers + 4, 1, cy), f32),
            pltpu.VMEM((3, 2, cx, cy), f32),
            pltpu.VMEM((3, 2, cx, cy), f32),
            pltpu.VMEM((5, 4, cx, cy), f32),
            dma((2, n_gy - 1)),
            dma((2, n_gy - 1)),
            dma((7,)),
            dma((4, 2)),
            dma((4, 2)),
            dma((3, 2)),
            dma((3, 2)),
        ],
        compiler_params=pltpu.CompilerParams(
            collective_id=0, has_side_effects=True, vmem_limit_bytes=60 * 1024 * 1024
        ),
        name="window",
    )(holder, soil_table.T, slab, factors, soil_class, cot)
    shape = cotangent.shape
    return state2.reshape(shape), adjoint0.reshape(shape)


def solution(mesh):
    placed = (
        P(None, None, "gx", "gy"),
        P(None, None, "gx", "gy"),
        P(),
        P("gx", "gy"),
        P(),
        P(None, None, "gx", "gy"),
    )
    return jax.shard_map(
        functools.partial(on_device, mesh.shape["gx"], mesh.shape["gy"]),
        mesh=mesh,
        in_specs=placed,
        out_specs=(P(None, None, "gx", "gy"), P(None, None, "gx", "gy")),
        check_vma=False,
    )
```

time: 36.1 us -> 31 us (0.86)
  Pallas kernels: 29.9 us -> 26.4 us
  local copies, waits for them, and re-layouts: 5.36 us -> 3.75 us
    pallas_call x1, Pallas kernels: 29.9 us -> 26.4 us  [on_device(): pl.pallas_call(functools.partial(window, n_gx, n_gy, nz), out_shape=(out,...]
    unnamed x15 -> x6, local copies, waits for them, and re-layouts: 5.27 us -> 3.07 us
    broadcast_in_dim x1, local copies, waits for them, and re-layouts: 0.01 us -> 0.6 us  [on_device(): factors = jnp.broadcast_to(factors[None], (cx, cy))]
where the time goes in v1:
time: 31 us; the launch traced here: 30.8 us
  Pallas kernels  26.4 us (85%)
  local copies, waits for them, and re-layouts  3.75 us (12%)
  between operations  0.66 us (2%)
    pallas_call x1, Pallas kernels, on_device(): pl.pallas_call(functools.partial(window, n_gx, n_gy, nz), out_shape=(out,...  26.4 us
    unnamed x6, local copies, waits for them, and re-layouts  3.07 us

profile of v1, /device:TPU:0, one launch (start us, length us, event | category | flops | bytes accessed | tf_op | source)
XLA Modules:
  0.0 30.8 jit_solution(13724953419873995226)
XLA Ops:
  0.6 0.0 copy-start.1
  0.6 0.6 %copy-done.1 = bf16[2,32,1,1]{1,0,3,2:T(2,128)(2,1)S(1)} copy-done((bf16[2,32,1,1]{1,0,3,2:T(2,128)(2,1)S(1)}, bf16[2,32,1,1]{1,0,3,2:T(2,128)(2,1)}, u32[]{:S(2)}) %copy-start.1) | copy-done | bytes 152
  1.3 0.1 convert_element_type.5
  1.4 0.6 %broadcast_in_dim.2.scale = f32[8,128]{1,0:T(8,128)} broadcast(f32[128]{0:T(128)S(1)} %pad_convert_fusion), dimensions={1} | broadcast | bytes 4608 | tf_op jit(solution)/shard_map/broadcast_in_dim | solution.py:406
  2.0 26.4 %window.1 = (f32[64,8,128]{2,1,0:T(8,128)}, f32[64,8,128]{2,1,0:T(8,128)}) custom-call(s32[4]{0:T(128)} %holder_in.1, f32[4,12]{1,0:T(4,128)} %bitcast.11, bf16[32,16,128]{2,1,0:T(8,128)(2,1)} %bitcast.10, f32[8,128]{1,0:T(8,128)} %broadcast_in_dim.2.scale, s32[8,128]{1,0:T(8,128)} %classes_in.1, f32[64,8,128]{2,1,0:T(8,128)} %bitcast.7), custom_call_target="tpu_custom_call" | custom-call | tf_op jit(solution)/shard_map/window/pallas_call | solution.py:412
  28.4 0.0 copy-start
  28.4 1.7 %copy.10 = f32[2,32,8,128]{3,2,1,0:T(8,128)} copy(f32[2,32,8,128]{3,2,1,0:T(8,128)} %bitcast.9) | data formatting | bytes 524288
  30.1 0.0 copy-done
  30.1 0.7 %copy.11 = f32[2,32,8,128]{3,2,1,0:T(8,128)} copy(f32[2,32,8,128]{3,2,1,0:T(8,128)S(1)} %bitcast.8) | data formatting | bytes 524288
  (1 shorter events, 0.0 us)
Async XLA Ops:
  0.6 0.7 %copy-start.1 = (bf16[2,32,1,1]{1,0,3,2:T(2,128)(2,1)S(1)}, bf16[2,32,1,1]{1,0,3,2:T(2,128)(2,1)}, u32[]{:S(2)}) copy-start(bf16[2,32,1,1]{1,0,3,2:T(2,128)(2,1)} %param.9) | copy-start | bytes 388
  28.4 1.7 %copy-start = (f32[64,8,128]{2,1,0:T(8,128)S(1)}, f32[64,8,128]{2,1,0:T(8,128)}, u32[]{:S(2)}) copy-start(f32[64,8,128]{2,1,0:T(8,128)} %get-tuple-element.17) | copy-start | bytes 786436

commit v2 on v1

--- a/solution.py
+++ b/solution.py
@@ -14,11 +14,12 @@
 def window(
     n_gx, n_gy, nz, holder_in, table_in, slab_in, scale, classes_in, cot, out2, outs,
     holder, table, classes, slots, sslots, m0, m1, g0, g1, left0, right0, near0, near1,
-    xs, xr, ys, yr, coef, gsend, grecv, lsem, xsend, xrecv, ysend, yrecv,
+    gnear, held2, helds, xs, xr, ys, yr, coef,
+    gsend, grecv, lsem, osem, xsend, xrecv, ysend, yrecv,
 ):
     gx, gy = lax.axis_index("gx"), lax.axis_index("gy")
     cx, cy = classes.shape
-    half = n_gy // 2
+    chips, hz = n_gy // 2, nz // 2
     partner = gy + 1 - 2 * lax.rem(gy, 2)
     lane = lax.broadcasted_iota(jnp.int32, (cx, cy), 1)
     sub = lax.broadcasted_iota(jnp.int32, (cx, cy), 0)
@@ -62,7 +63,11 @@
         @pl.when(jnp.logical_not(y_has[side]))
         def _():
             for e in range(3):
-                yr[e, side] = jnp.zeros((cx, cy), jnp.float32)
+                for half in range(2):
+                    yr[e, half, side] = jnp.zeros((cx, cy), jnp.float32)
+
+    def row_of(f, z):
+        return z + f * hz + lax.div(z, hz) * hz
 
     for ref in (m0, m1, g0, g1):
         for q in range(ref.shape[0]):
@@ -86,9 +91,9 @@
 
     blank = (jnp.zeros((cx, cy), jnp.float32),) * 2
 
-    def by_chunks(layers, size, work, store, carry):
+    def by_chunks(first, layers, size, work, store, carry):
         def chunk(i, carry):
-            zs = [i * size + j for j in range(size)]
+            zs = [first + i * size + j for j in range(size)]
             found = [work(z) for z in zs]
             for z, value in zip(zs, found):
                 carry = store(z, value, carry)
@@ -109,56 +114,63 @@
 
     def put_cot(z, values, carry):
         for f in range(2):
-            edges_x(COT, f * nz + z, values[f])
-            carry = edges_y(carry, f * nz + z, values[f])
+            edges_x(COT, row_of(f, z), values[f])
+            carry = edges_y(carry, row_of(f, z), values[f])
         return carry
 
     for copy in cots:
         copy.wait()
-    carry = by_chunks(nz, 8, lambda z: [g0[f, z + 1] for f in range(2)], put_cot, blank)
+    carry = by_chunks(0, nz, 8, lambda z: [g0[f, z + 1] for f in range(2)], put_cot, blank)
     for k in range(4):
         carry = edges_y(carry, 2 * nz + k, coef[0, k])
-    ys[0, 0], ys[0, 1] = carry
-
-    def x_copy(e, side):
+    ys[0, 0, 0], ys[0, 0, 1] = carry
+
+    def x_copy(e, half, side):
         there = gx - 1 if side == 0 else gx + 1
+        part = pl.ds(0, 2 * nz + 4) if e == COT else pl.ds(half * nz, nz)
         return pltpu.make_async_remote_copy(
-            src_ref=xs.at[e, side], dst_ref=xr.at[e, 1 - side],
-            send_sem=xsend.at[e, side], recv_sem=xrecv.at[e, 1 - side],
+            src_ref=xs.at[e, side, part], dst_ref=xr.at[e, 1 - side, part],
+            send_sem=xsend.at[e, half, side], recv_sem=xrecv.at[e, half, 1 - side],
             device_id=(there, gy), device_id_type=MESH,
         )
 
-    def y_copy(e, side):
+    y_of = {COT: 0, ST1: 1, ADJ: 2}
+
+    def y_copy(e, half, side):
         there = gy - 1 if side == 0 else gy + 1
+        i = y_of[e]
         return pltpu.make_async_remote_copy(
-            src_ref=ys.at[e, side], dst_ref=yr.at[e, 1 - side],
-            send_sem=ysend.at[e, side], recv_sem=yrecv.at[e, 1 - side],
+            src_ref=ys.at[i, half, side], dst_ref=yr.at[i, half, 1 - side],
+            send_sem=ysend.at[i, half, side], recv_sem=yrecv.at[i, half, 1 - side],
             device_id=(gx, there), device_id_type=MESH,
         )
 
-    def for_sides(make, has, e, act):
-        for side in range(2):
-            @pl.when(has[side])
-            def _():
-                act(make(e, side))
-
-    def start(c):
-        c.start()
-
-    def arrived(make, has, e):
-        for side in range(2):
-            @pl.when(has[side])
-            def _():
-                make(e, 1 - side).wait_recv()
-
-    def block_copies(index, slot, there):
-        src, ssrc = slots.at[slot], sslots.at[slot]
+    def each(e, half, act, mirrored=False):
+        for make, has in ((x_copy, x_has), (y_copy, y_has)):
+            if make is y_copy and e not in y_of:
+                continue
+            for side in range(2):
+                @pl.when(has[side])
+                def _():
+                    act(make(e, half, 1 - side if mirrored else side))
+
+    def start(e, half):
+        each(e, half, lambda c: c.start())
+
+    def arrived(e, half):
+        each(e, half, lambda c: c.wait_recv(), mirrored=True)
+
+    def block_copies(index, slot, there, field):
+        part = pl.ds(field * hz, hz)
+        pieces = [(slots.at[slot, part], field)]
+        if field == 0:
+            pieces.append((sslots.at[slot], 2))
         return [
             pltpu.make_async_remote_copy(
-                src_ref=a, dst_ref=b.at[slot], send_sem=gsend.at[i, index],
+                src_ref=ref, dst_ref=ref, send_sem=gsend.at[i, index],
                 recv_sem=grecv.at[i, index], device_id=(gx, there), device_id_type=MESH,
             )
-            for i, (a, b) in enumerate(((src, slots), (ssrc, sslots)))
+            for ref, i in pieces
         ]
 
     greeted = n_gy - 1 + jnp.where(gx > 0, 1, 0) + jnp.where(gx < n_gx - 1, 1, 0)
@@ -166,23 +178,72 @@
         copy.wait()
     pl.semaphore_wait(barrier, greeted)
 
-    sent = []
-    for k in range(1, half):
-        sent += block_copies(k, gy, lax.rem(gy + 2 * k, n_gy))
-    sent += block_copies(0, gy, partner)
-    for c in sent:
-        c.start()
-    for_sides(y_copy, y_has, 0, start)
-    for_sides(x_copy, x_has, COT, start)
-    for k in range(1, half):
-        for c in sent[2 * k - 2 : 2 * k]:
+    start(COT, 0)
+    direct = [
+        [block_copies(k, gy, lax.rem(gy + 2 * k, n_gy), field) for k in range(1, chips)]
+        for field in range(2)
+    ]
+    beside = [block_copies(0, gy, partner, field) for field in range(2)]
+    for field in range(2):
+        for copies in direct[field] + [beside[field]]:
+            for c in copies:
+                c.start()
+    sent = direct[0] + direct[1] + beside
+    onward = [[], []]
+
+    def pass_on(field):
+        for k in range(1, chips):
+            for c in direct[field][k - 1]:
+                c.wait_recv()
+            copies = block_copies(chips - 1 + k, lax.rem(gy - 2 * k + n_gy, n_gy), partner, field)
+            for c in copies:
+                c.start()
+            onward[field].append(copies)
+
+    arrived(COT, 0)
+
+    def beside_x(value, low, high):
+        return (
+            jnp.where(first_row, low, pltpu.roll(value, 1, 0)),
+            jnp.where(last_row, high, pltpu.roll(value, cx - 1, 0)),
+        )
+
+    def beside_y(value, low, high, slot):
+        return (
+            jnp.where(first_lane, to_lane(low, slot, 0), pltpu.roll(value, 1, 1)),
+            jnp.where(last_lane, to_lane(high, slot, cy - 1), pltpu.roll(value, cy - 1, 1)),
+        )
+
+    for k in range(4):
+        value = coef[0, k]
+        row = 2 * nz + k
+        near = beside_x(value, xr[COT, 0, row], xr[COT, 1, row]) + beside_y(
+            value, yr[0, 0, 0], yr[0, 0, 1], row
+        )
+        for d in range(4):
+            coef[1 + d, k] = near[d]
+
+    def rows(e, row):
+        return xr[e, 0, row], xr[e, 1, row]
+
+    def field_near(e, f, z, value):
+        row, i, half = row_of(f, z), y_of[e], 0 if e == COT else lax.div(z, hz)
+        return beside_x(value, *rows(e, row)) + beside_y(value, yr[i, half, 0], yr[i, half, 1], row)
+
+    def put_cot_near(z, found, _):
+        for f in range(2):
+            for d in range(4):
+                gnear[4 * f + d, z] = found[f][d]
+        return 0
+
+    by_chunks(0, nz, 4, lambda z: [field_near(COT, f, z, g0[f, z + 1]) for f in range(2)], put_cot_near, 0)
+
+    for field in range(2):
+        pass_on(field)
+    sent += onward[0] + onward[1]
+    for copies in beside + onward[0] + onward[1]:
+        for c in copies:
             c.wait_recv()
-        onward = block_copies(half - 1 + k, lax.rem(gy - 2 * k + n_gy, n_gy), partner)
-        for c in onward:
-            c.start()
-        sent += onward
-    for c in sent[2 * half - 2 :]:
-        c.wait_recv()
 
     def strength(u):
         return 1.5 + jnp.tanh(u)
@@ -201,15 +262,32 @@
 
         return pair
 
-    def put_own(p, values, _):
+    def put_own(p, found, _):
+        values, strengths = found
         for j in range(2):
             l = 2 * p + j
-            m0[l // nz, lax.rem(l, nz) + 1] = values[j]
-            edges_x(ST0, l, values[j])
+            f, z = lax.div(l, nz), lax.rem(l, nz)
+            m0[f, z + 1] = values[j]
+            edges_x(ST0, row_of(f, z), values[j])
+            if strengths:
+                m0[2, z + 1] = strengths[j]
+                m0[3, z + 1] = 0.75 + 0.5 * strengths[j]
         return 0
 
-    by_chunks(nz, 8, pair_of(gy, 1.0), put_own, 0)
-    for_sides(x_copy, x_has, ST0, start)
+    def own_of(f):
+        pair = pair_of(gy, 1.0)
+
+        def work(p):
+            values = pair(p)
+            return values, [strength(v) for v in values] if f == 0 else None
+
+        return work
+
+    quarter = hz // 2
+    for half in range(2):
+        for f in range(2):
+            by_chunks(f * hz + half * quarter, quarter, 8, own_of(f), put_own, 0)
+        start(ST0, half)
 
     before = pair_of(jnp.maximum(gy - 1, 0), jnp.where(gy > 0, 1.0, 0.0))
     after = pair_of(jnp.minimum(gy + 1, n_gy - 1), jnp.where(gy < n_gy - 1, 1.0, 0.0))
@@ -221,55 +299,20 @@
                 ref[l // nz, lax.rem(l, nz)] = pair[j]
         return 0
 
-    by_chunks(nz, 4, lambda p: (before(p), after(p)), put_sides, 0)
-
-    def put_strength(z, s, _):
-        m0[2, z + 1] = s
-        m0[3, z + 1] = 0.75 + 0.5 * s
-        return 0
-
-    by_chunks(nz, 8, lambda z: strength(m0[0, z + 1]), put_strength, 0)
-
-    arrived(y_copy, y_has, 0)
-    arrived(x_copy, x_has, COT)
-
-    def beside_x(value, low, high):
-        return (
-            jnp.where(first_row, low, pltpu.roll(value, 1, 0)),
-            jnp.where(last_row, high, pltpu.roll(value, cx - 1, 0)),
-        )
-
-    def beside_y(value, low, high, slot):
-        return (
-            jnp.where(first_lane, to_lane(low, slot, 0), pltpu.roll(value, 1, 1)),
-            jnp.where(last_lane, to_lane(high, slot, cy - 1), pltpu.roll(value, cy - 1, 1)),
-        )
-
-    for k in range(4):
-        value = coef[0, k]
-        row = 2 * nz + k
-        near = beside_x(value, xr[COT, 0, row], xr[COT, 1, row]) + beside_y(
-            value, yr[0, 0], yr[0, 1], row
-        )
-        for d in range(4):
-            coef[1 + d, k] = near[d]
-
-    def rows(e, row):
-        return xr[e, 0, row], xr[e, 1, row]
+    by_chunks(0, nz, 4, lambda p: (before(p), after(p)), put_sides, 0)
 
     def state_near(level, z):
         m, e = (m0, ST0) if level == 0 else (m1, ST1)
         found = []
         for q in range(2):
             value = m[q, z + 1]
-            near = beside_x(value, *rows(e, q * nz + z))
             if level == 0:
-                near += (
+                near = beside_x(value, *rows(e, row_of(q, z))) + (
                     pltpu.roll(jnp.where(last_lane, left0[q, z], value), 1, 1),
                     pltpu.roll(jnp.where(first_lane, right0[q, z], value), cy - 1, 1),
                 )
             else:
-                near += beside_y(value, yr[1, 0], yr[1, 1], q * nz + z)
+                near = field_near(ST1, q, z, value)
             found.append(near)
         found.append([strength(u) for u in found[0]])
         return found
@@ -303,18 +346,16 @@
         return u + 0.5 * water, t + 0.5 * energy
 
     def backward(level, z, near):
-        m, g, ge, gy_slot = (m0, g1, ADJ, 2) if level == 0 else (m1, g0, COT, 0)
+        m, g = (m0, g1) if level == 0 else (m1, g0)
         us, ts, ss = near
         u, t, s, h = (m[q, z + 1] for q in range(4))
         c0, c1, c2, c3 = (coef[0, k] for k in range(4))
         kw, dtv, lamb, kv = c0 * s, c1 * h, c2 * h, c3 * s
-        gws, ges = [], []
-        for q, into in ((0, gws), (1, ges)):
-            value = g[q, z + 1]
-            into.append(value)
-            into += beside_x(value, *rows(ge, q * nz + z))
-            into += beside_y(value, yr[gy_slot, 0], yr[gy_slot, 1], q * nz + z)
-        w, e = gws[0], ges[0]
+        w, e = g[0, z + 1], g[1, z + 1]
+        if level == 0:
+            gws, ges = field_near(ADJ, 0, z, w), field_near(ADJ, 1, z, e)
+        else:
+            gws, ges = ([gnear[4 * f + d, z] for d in range(4)] for f in range(2))
         pu = pt = q1 = q2 = q3 = q4 = 0.0
         for zn in (z, z + 2):
             du, dt = m[0, zn] - u, m[1, zn] - t
@@ -327,7 +368,7 @@
             sn = ss[d]
             hn = 0.75 + 0.5 * sn
             du, dt = us[d] - u, ts[d] - t
-            dw, de = gws[1 + d] - w, ges[1 + d] - e
+            dw, de = gws[d] - w, ges[d] - e
             pu += (kw + coef[1 + d, 0] * sn) * dw + (kv + coef[1 + d, 3] * sn) * de
             pt += (dtv + coef[1 + d, 1] * hn) * dw + (lamb + coef[1 + d, 2] * hn) * de
             q1, q2, q3, q4 = q1 + du * dw, q2 + du * de, q3 + dt * dw, q4 + dt * de
@@ -339,11 +380,9 @@
     def put_edges(e, ref, z, pair, carry):
         for f in range(2):
             ref[f, z + 1] = pair[f]
-            edges_x(e, f * nz + z, pair[f])
-            carry = edges_y(carry, f * nz + z, pair[f])
+            edges_x(e, row_of(f, z), pair[f])
+            carry = edges_y(carry, row_of(f, z), pair[f])
         return carry
-
-    arrived(x_copy, x_has, ST0)
 
     def work1(z):
         near = state_near(0, z)
@@ -357,11 +396,10 @@
         m1[3, z + 1] = 0.75 + 0.5 * s
         return put_edges(ST1, m1, z, pair, carry)
 
-    ys[1, 0], ys[1, 1] = by_chunks(nz, 4, work1, put1, blank)
-    for_sides(x_copy, x_has, ST1, start)
-    for_sides(y_copy, y_has, 1, start)
-    arrived(x_copy, x_has, ST1)
-    arrived(y_copy, y_has, 1)
+    for half in range(2):
+        arrived(ST0, half)
+        ys[1, half, 0], ys[1, half, 1] = by_chunks(half * hz, hz, 4, work1, put1, blank)
+        start(ST1, half)
 
     def work2(z):
         near = state_near(1, z)
@@ -372,9 +410,10 @@
         keep_near(near1, z, near)
         return put_edges(ADJ, g1, z, pair, carry)
 
-    ys[2, 0], ys[2, 1] = by_chunks(nz, 4, work2, put2, blank)
-    for_sides(x_copy, x_has, ADJ, start)
-    for_sides(y_copy, y_has, 2, start)
+    for half in range(2):
+        arrived(ST1, half)
+        ys[2, half, 0], ys[2, half, 1] = by_chunks(half * hz, hz, 4, work2, put2, blank)
+        start(ADJ, half)
 
     def put_out(ref):
         def put(z, pair, _):
@@ -383,17 +422,53 @@
             return 0
         return put
 
-    by_chunks(nz, 4, lambda z: forward(1, z, kept_near(near1, z)), put_out(out2), 0)
-    arrived(x_copy, x_has, ADJ)
-    arrived(y_copy, y_has, 2)
-    by_chunks(nz, 4, lambda z: backward(0, z, kept_near(near0, z)), put_out(outs), 0)
-
-    for c in sent:
-        c.wait_send()
-    for e in range(4):
-        for_sides(x_copy, x_has, e, lambda c: c.wait_send())
-    for e in range(3):
-        for_sides(y_copy, y_has, e, lambda c: c.wait_send())
+    written = []
+
+    def write(i, held, out, half):
+        for f in range(2):
+            part = pl.ds(f * nz + half * hz, hz)
+            copy = pltpu.make_async_copy(held.at[part], out.at[part], osem.at[i, half, f])
+            copy.start()
+            written.append(copy)
+
+    for half in range(2):
+        by_chunks(
+            half * hz, hz, 4, lambda z: forward(1, z, kept_near(near1, z)), put_out(held2), 0
+        )
+        write(0, held2, out2, half)
+    for half in range(2):
+        arrived(ADJ, half)
+        by_chunks(
+            half * hz, hz, 4, lambda z: backward(0, z, kept_near(near0, z)), put_out(helds), 0
+        )
+        write(1, helds, outs, half)
+
+    for copies in sent:
+        for c in copies:
+            c.wait_send()
+    each(COT, 0, lambda c: c.wait_send())
+    for e in (ST0, ST1, ADJ):
+        for half in range(2):
+            each(e, half, lambda c: c.wait_send())
+    for copy in written:
+        copy.wait()
+
+
+def hand_over(a, b, a_out, b_out, sems):
+    layers, parts = a.shape[0], sems.shape[1]
+    copies = [
+        pltpu.make_async_copy(
+            src.at[pl.ds(j * layers // parts, layers // parts)],
+            dst.at[pl.ds(j * layers // parts, layers // parts)],
+            sems.at[i, j],
+        )
+        for i, (src, dst) in enumerate(((a, a_out), (b, b_out)))
+        for j in range(parts)
+    ]
+    for c in copies:
+        c.start()
+    for c in copies:
+        c.wait()
 
 
 def on_device(n_gx, n_gy, stored_slab, block_scales, holder, soil_class, soil_table, cotangent):
@@ -413,7 +488,7 @@
         functools.partial(window, n_gx, n_gy, nz),
         out_shape=(out, out),
         in_specs=[hbm, hbm, hbm, vmem, hbm, hbm],
-        out_specs=(vmem, vmem),
+        out_specs=(hbm, hbm),
         scratch_shapes=[
             pltpu.SMEM(holder.shape, jnp.int32),
             pltpu.SMEM(soil_table.shape[::-1], f32),
@@ -428,24 +503,37 @@
             pltpu.VMEM((2, nz, cx, cy), f32),
             pltpu.VMEM((12, nz, cx, cy), f32),
             pltpu.VMEM((12, nz, cx, cy), f32),
+            pltpu.VMEM((8, nz, cx, cy), f32),
+            pltpu.VMEM((layers, cx, cy), f32),
+            pltpu.VMEM((layers, cx, cy), f32),
             pltpu.VMEM((4, 2, layers + 4, 1, cy), f32),
             pltpu.VMEM((4, 2, layers + 4, 1, cy), f32),
-            pltpu.VMEM((3, 2, cx, cy), f32),
-            pltpu.VMEM((3, 2, cx, cy), f32),
+            pltpu.VMEM((3, 2, 2, cx, cy), f32),
+            pltpu.VMEM((3, 2, 2, cx, cy), f32),
             pltpu.VMEM((5, 4, cx, cy), f32),
-            dma((2, n_gy - 1)),
-            dma((2, n_gy - 1)),
+            dma((3, n_gy - 1)),
+            dma((3, n_gy - 1)),
             dma((7,)),
-            dma((4, 2)),
-            dma((4, 2)),
-            dma((3, 2)),
-            dma((3, 2)),
+            dma((2, 2, 2)),
+            dma((4, 2, 2)),
+            dma((4, 2, 2)),
+            dma((3, 2, 2)),
+            dma((3, 2, 2)),
         ],
         compiler_params=pltpu.CompilerParams(
             collective_id=0, has_side_effects=True, vmem_limit_bytes=60 * 1024 * 1024
         ),
         name="window",
     )(holder, soil_table.T, slab, factors, soil_class, cot)
+    state2, adjoint0 = pl.pallas_call(
+        hand_over,
+        out_shape=(out, out),
+        in_specs=[hbm, hbm],
+        out_specs=(hbm, hbm),
+        scratch_shapes=[dma((2, 4))],
+        compiler_params=pltpu.CompilerParams(vmem_limit_bytes=60 * 1024 * 1024),
+        name="hand_over",
+    )(state2, adjoint0)
     shape = cotangent.shape
     return state2.reshape(shape), adjoint0.reshape(shape)
 

time: 31 us -> 43 us (1.39)
  Pallas kernels: 26.4 us -> 40.8 us
  local copies, waits for them, and re-layouts: 3.75 us -> 1.33 us
    pallas_call x0 -> x1, Pallas kernels: none -> 17.1 us  [on_device(): pl.pallas_call(hand_over, out_shape=(out, out), in_specs=[hbm, hbm], out_...]
    pallas_call x1, Pallas kernels: 26.4 us -> 23.7 us  [on_device(): pl.pallas_call(functools.partial(window, n_gx, n_gy, nz), out_shape=(out,...]
    unnamed x6 -> x2, local copies, waits for them, and re-layouts: 3.07 us -> 0.65 us
where the time goes in v2:
time: 43 us; the launch traced here: 42.8 us
  Pallas kernels  40.8 us (95%)
  local copies, waits for them, and re-layouts  1.33 us (3%)
  between operations  0.65 us (2%)
    pallas_call x1, Pallas kernels, on_device(): pl.pallas_call(functools.partial(window, n_gx, n_gy, nz), out_shape=(out,...  23.7 us
    pallas_call x1, Pallas kernels, on_device(): pl.pallas_call(hand_over, out_shape=(out, out), in_specs=[hbm, hbm], out_...  17.1 us

profile of v2, /device:TPU:0, one launch (start us, length us, event | category | flops | bytes accessed | tf_op | source)
XLA Modules:
  0.0 42.8 jit_solution(18233672233010379627)
XLA Ops:
  0.6 0.0 copy-start
  0.6 0.6 %copy-done = bf16[2,32,1,1]{1,0,3,2:T(2,128)(2,1)S(1)} copy-done((bf16[2,32,1,1]{1,0,3,2:T(2,128)(2,1)S(1)}, bf16[2,32,1,1]{1,0,3,2:T(2,128)(2,1)}, u32[]{:S(2)}) %copy-start) | copy-done | bytes 152
  1.3 0.1 convert_element_type.5
  1.4 0.6 %broadcast_in_dim.2.scale = f32[8,128]{1,0:T(8,128)} broadcast(f32[128]{0:T(128)S(1)} %pad_convert_fusion), dimensions={1} | broadcast | bytes 4608 | tf_op jit(solution)/shard_map/broadcast_in_dim | solution.py:481
  2.0 23.7 %window.1 = (f32[64,8,128]{2,1,0:T(8,128)}, f32[64,8,128]{2,1,0:T(8,128)}) custom-call(s32[4]{0:T(128)} %holder_in.1, f32[4,12]{1,0:T(4,128)} %bitcast.9, bf16[32,16,128]{2,1,0:T(8,128)(2,1)} %bitcast.8, f32[8,128]{1,0:T(8,128)} %broadcast_in_dim.2.scale, s32[8,128]{1,0:T(8,128)} %classes_in.1, f32[64,8,128]{2,1,0:T(8,128)} %bitcast.7), custom_call_target="tpu_custom_call" | custom-call | tf_op jit(solution)/shard_map/window/pallas_call | solution.py:487
  25.7 17.1 %hand_over.1 = (f32[64,8,128]{2,1,0:T(8,128)}, f32[64,8,128]{2,1,0:T(8,128)}) custom-call(f32[64,8,128]{2,1,0:T(8,128)} %get-tuple-element.18.a, f32[64,8,128]{2,1,0:T(8,128)} %get-tuple-element.19.b), custom_call_target="tpu_custom_call" | custom-call | tf_op jit(solution)/shard_map/hand_over/pallas_call | solution.py:528
  (1 shorter events, 0.0 us)
Async XLA Ops:
  0.6 0.7 %copy-start = (bf16[2,32,1,1]{1,0,3,2:T(2,128)(2,1)S(1)}, bf16[2,32,1,1]{1,0,3,2:T(2,128)(2,1)}, u32[]{:S(2)}) copy-start(bf16[2,32,1,1]{1,0,3,2:T(2,128)(2,1)} %param.9) | copy-start | bytes 388

commit v3 on v2

--- a/solution.py
+++ b/solution.py
@@ -13,7 +13,7 @@
 
 def window(
     n_gx, n_gy, nz, holder_in, table_in, slab_in, scale, classes_in, cot, out2, outs,
-    holder, table, classes, slots, sslots, m0, m1, g0, g1, left0, right0, near0, near1,
+    holder, table, classes, scales, spread, slots, sslots, m0, m1, g0, g1, left0, right0, near0, near1,
     gnear, held2, helds, xs, xr, ys, yr, coef,
     gsend, grecv, lsem, osem, xsend, xrecv, ysend, yrecv,
 ):
@@ -43,16 +43,51 @@
     ]
     own = [
         pltpu.make_async_copy(slab_in, slots.at[gy], lsem.at[3]),
-        pltpu.make_async_copy(scale, sslots.at[gy], lsem.at[4]),
     ]
+    scaling = pltpu.make_async_copy(scale, scales, lsem.at[4])
     cots = [
         pltpu.make_async_copy(
             cot.at[pl.ds(f * nz, nz)], g0.at[f, pl.ds(1, nz)], lsem.at[5 + f]
         )
         for f in range(2)
     ]
-    for copy in small + own + cots:
+    for copy in own + [scaling] + small + cots:
         copy.start()
+    greeted = n_gy - 1 + jnp.where(gx > 0, 1, 0) + jnp.where(gx < n_gx - 1, 1, 0)
+    pl.semaphore_wait(barrier, greeted)
+
+    def block_copies(index, slot, there, field):
+        part = pl.ds(field * hz, hz)
+        src = slab_in.at[part] if slot is gy else slots.at[slot, part]
+        pieces = [(src, slots.at[slot, part], field)]
+        if field == 1:
+            pieces.append((sslots.at[slot], sslots.at[slot], 2))
+        return [
+            pltpu.make_async_remote_copy(
+                src_ref=src, dst_ref=dst, send_sem=gsend.at[i, index],
+                recv_sem=grecv.at[i, index], device_id=(gx, there), device_id_type=MESH,
+            )
+            for src, dst, i in pieces
+        ]
+
+    direct = [
+        [block_copies(k, gy, lax.rem(gy + 2 * k, n_gy), field) for k in range(1, chips)]
+        for field in range(2)
+    ]
+    beside = [block_copies(0, gy, partner, field) for field in range(2)]
+    for field in range(2):
+        for copies in direct[field] + [beside[field]]:
+            copies[0].start()
+    spread[...] = jnp.zeros((cx, cy), jnp.float32)
+    scaling.wait()
+    spread[0:2, 0:nz] = scales[...].astype(jnp.float32)
+    sslots[gy] = jnp.where(
+        lane < nz,
+        jnp.broadcast_to(spread[0:1], (cx, cy)),
+        pltpu.roll(jnp.broadcast_to(spread[1:2], (cx, cy)), nz, 1),
+    )
+    for copies in direct[1] + [beside[1]]:
+        copies[1].start()
 
     for side in range(2):
         @pl.when(jnp.logical_not(x_has[side]))
@@ -160,34 +195,7 @@
     def arrived(e, half):
         each(e, half, lambda c: c.wait_recv(), mirrored=True)
 
-    def block_copies(index, slot, there, field):
-        part = pl.ds(field * hz, hz)
-        pieces = [(slots.at[slot, part], field)]
-        if field == 0:
-            pieces.append((sslots.at[slot], 2))
-        return [
-            pltpu.make_async_remote_copy(
-                src_ref=ref, dst_ref=ref, send_sem=gsend.at[i, index],
-                recv_sem=grecv.at[i, index], device_id=(gx, there), device_id_type=MESH,
-            )
-            for ref, i in pieces
-        ]
-
-    greeted = n_gy - 1 + jnp.where(gx > 0, 1, 0) + jnp.where(gx < n_gx - 1, 1, 0)
-    for copy in own:
-        copy.wait()
-    pl.semaphore_wait(barrier, greeted)
-
     start(COT, 0)
-    direct = [
-        [block_copies(k, gy, lax.rem(gy + 2 * k, n_gy), field) for k in range(1, chips)]
-        for field in range(2)
-    ]
-    beside = [block_copies(0, gy, partner, field) for field in range(2)]
-    for field in range(2):
-        for copies in direct[field] + [beside[field]]:
-            for c in copies:
-                c.start()
     sent = direct[0] + direct[1] + beside
     onward = [[], []]
 
@@ -200,6 +208,9 @@
                 c.start()
             onward[field].append(copies)
 
+    for field in range(2):
+        pass_on(field)
+
     arrived(COT, 0)
 
     def beside_x(value, low, high):
@@ -238,12 +249,12 @@
 
     by_chunks(0, nz, 4, lambda z: [field_near(COT, f, z, g0[f, z + 1]) for f in range(2)], put_cot_near, 0)
 
-    for field in range(2):
-        pass_on(field)
     sent += onward[0] + onward[1]
     for copies in beside + onward[0] + onward[1]:
         for c in copies:
             c.wait_recv()
+    for copy in own:
+        copy.wait()
 
     def strength(u):
         return 1.5 + jnp.tanh(u)
@@ -454,20 +465,28 @@
         copy.wait()
 
 
-def hand_over(a, b, a_out, b_out, sems):
-    layers, parts = a.shape[0], sems.shape[1]
-    copies = [
+def hand_over(a, b, a_out, b_out, held, in_sems, out_sems):
+    parts = in_sems.shape[1]
+    size = a.shape[0] // parts
+    pieces = [(i, j) for j in range(parts) for i in range(2)]
+    reads = [
         pltpu.make_async_copy(
-            src.at[pl.ds(j * layers // parts, layers // parts)],
-            dst.at[pl.ds(j * layers // parts, layers // parts)],
-            sems.at[i, j],
-        )
-        for i, (src, dst) in enumerate(((a, a_out), (b, b_out)))
-        for j in range(parts)
+            (a, b)[i].at[pl.ds(j * size, size)], held.at[i, pl.ds(j * size, size)], in_sems.at[i, j]
+        )
+        for i, j in pieces
     ]
-    for c in copies:
+    writes = [
+        pltpu.make_async_copy(
+            held.at[i, pl.ds(j * size, size)], (a_out, b_out)[i].at[pl.ds(j * size, size)], out_sems.at[i, j]
+        )
+        for i, j in pieces
+    ]
+    for c in reads:
         c.start()
-    for c in copies:
+    for read, write in zip(reads, writes):
+        read.wait()
+        write.start()
+    for c in writes:
         c.wait()
 
 
@@ -477,22 +496,22 @@
     assert n_gy % 2 == 0 and layers + 4 <= cy
     f32 = jnp.float32
     slab = stored_slab.reshape(nz, 2 * cx, cy)
-    factors = jnp.zeros((cy,), f32).at[:layers].set(block_scales.reshape(layers).astype(f32))
-    factors = jnp.broadcast_to(factors[None], (cx, cy))
+    factors = jnp.transpose(block_scales, (2, 3, 0, 1)).reshape(2, nz)
     cot = cotangent.reshape(layers, cx, cy)
-    vmem = pl.BlockSpec(memory_space=pltpu.VMEM)
     hbm = pl.BlockSpec(memory_space=pltpu.HBM)
     out = jax.ShapeDtypeStruct((layers, cx, cy), f32)
     dma = pltpu.SemaphoreType.DMA
     state2, adjoint0 = pl.pallas_call(
         functools.partial(window, n_gx, n_gy, nz),
         out_shape=(out, out),
-        in_specs=[hbm, hbm, hbm, vmem, hbm, hbm],
+        in_specs=[hbm] * 6,
         out_specs=(hbm, hbm),
         scratch_shapes=[
             pltpu.SMEM(holder.shape, jnp.int32),
             pltpu.SMEM(soil_table.shape[::-1], f32),
             pltpu.VMEM((cx, cy), jnp.int32),
+            pltpu.VMEM((2, nz), jnp.bfloat16),
+            pltpu.VMEM((cx, cy), f32),
             pltpu.VMEM((n_gy, nz, 2 * cx, cy), jnp.bfloat16),
             pltpu.VMEM((n_gy, cx, cy), f32),
             pltpu.VMEM((4, nz + 2, cx, cy), f32),
@@ -530,7 +549,7 @@
         out_shape=(out, out),
         in_specs=[hbm, hbm],
         out_specs=(hbm, hbm),
-        scratch_shapes=[dma((2, 4))],
+        scratch_shapes=[pltpu.VMEM((2, layers, cx, cy), f32), dma((2, 4)), dma((2, 4))],
         compiler_params=pltpu.CompilerParams(vmem_limit_bytes=60 * 1024 * 1024),
         name="hand_over",
     )(state2, adjoint0)

time: 43 us -> 26.7 us (0.62)
  Pallas kernels: 40.8 us -> 25.9 us
  local copies, waits for them, and re-layouts: 1.33 us -> 0 us
    pallas_call x1, Pallas kernels: 17.1 us -> 1.83 us  [on_device(): pl.pallas_call(hand_over, out_shape=(out, out), in_specs=[hbm, hbm], out_...]
    unnamed x2 -> x0, local copies, waits for them, and re-layouts: 0.65 us -> none
    broadcast_in_dim x1 -> x0, local copies, waits for them, and re-layouts: 0.6 us -> none  [on_device(): factors = jnp.broadcast_to(factors[None], (cx, cy))]
where the time goes in v3:
time: 26.7 us; the launch traced here: 26.5 us
  Pallas kernels  25.9 us (97%)
  between operations  0.64 us (2%)
    pallas_call x1, Pallas kernels, on_device(): pl.pallas_call(functools.partial(window, n_gx, n_gy, nz), out_shape=(out,...  24 us
    pallas_call x1, Pallas kernels, on_device(): pl.pallas_call(hand_over, out_shape=(out, out), in_specs=[hbm, hbm], out_...  1.83 us

profile of v3, /device:TPU:0, one launch (start us, length us, event | category | flops | bytes accessed | tf_op | source)
XLA Modules:
  0.0 26.5 jit_solution(9381130076968941435)
XLA Ops:
  0.6 24.0 %window.1 = (f32[64,8,128]{2,1,0:T(8,128)}, f32[64,8,128]{2,1,0:T(8,128)}) custom-call(s32[4]{0:T(128)} %holder_in.1, f32[4,12]{1,0:T(4,128)} %bitcast.8, bf16[32,16,128]{2,1,0:T(8,128)(2,1)} %bitcast.7, bf16[2,32]{1,0:T(2,128)(2,1)} %bitcast.9, s32[8,128]{1,0:T(8,128)} %classes_in.1, f32[64,8,128]{2,1,0:T(8,128)} %bitcast.6), custom_call_target="tpu_custom_call" | custom-call | tf_op jit(solution)/shard_map/window/pallas_call | solution.py:504
  24.7 1.8 %hand_over.1 = (f32[64,8,128]{2,1,0:T(8,128)}, f32[64,8,128]{2,1,0:T(8,128)}) custom-call(f32[64,8,128]{2,1,0:T(8,128)} %get-tuple-element.6.a, f32[64,8,128]{2,1,0:T(8,128)} %get-tuple-element.7.b), custom_call_target="tpu_custom_call" | custom-call | tf_op jit(solution)/shard_map/hand_over/pallas_call | solution.py:547

commit v4 on v3

--- a/solution.py
+++ b/solution.py
@@ -241,13 +241,13 @@
         row, i, half = row_of(f, z), y_of[e], 0 if e == COT else lax.div(z, hz)
         return beside_x(value, *rows(e, row)) + beside_y(value, yr[i, half, 0], yr[i, half, 1], row)
 
-    def put_cot_near(z, found, _):
+    def keep_cot_near(z):
         for f in range(2):
+            found = field_near(COT, f, z, g0[f, z + 1])
             for d in range(4):
-                gnear[4 * f + d, z] = found[f][d]
-        return 0
-
-    by_chunks(0, nz, 4, lambda z: [field_near(COT, f, z, g0[f, z + 1]) for f in range(2)], put_cot_near, 0)
+                gnear[4 * f + d, z] = found[d]
+
+    by_chunks(0, nz, 4, keep_cot_near, lambda z, found, _: 0, 0)
 
     sent += onward[0] + onward[1]
     for copies in beside + onward[0] + onward[1]:
@@ -397,12 +397,12 @@
 
     def work1(z):
         near = state_near(0, z)
+        keep_near(near0, z, near)
         pair = forward(0, z, near)
-        return near, pair, strength(pair[0])
+        return pair, strength(pair[0])
 
     def put1(z, found, carry):
-        near, pair, s = found
-        keep_near(near0, z, near)
+        pair, s = found
         m1[2, z + 1] = s
         m1[3, z + 1] = 0.75 + 0.5 * s
         return put_edges(ST1, m1, z, pair, carry)
@@ -414,11 +414,10 @@
 
     def work2(z):
         near = state_near(1, z)
-        return near, backward(1, z, near)
-
-    def put2(z, found, carry):
-        near, pair = found
         keep_near(near1, z, near)
+        return backward(1, z, near)
+
+    def put2(z, pair, carry):
         return put_edges(ADJ, g1, z, pair, carry)
 
     for half in range(2):

time: 26.7 us -> 26.7 us (level)
  no operation moved by 1% of the time
where the time goes in v4:
time: 26.7 us; the launch traced here: 26.5 us
  Pallas kernels  25.8 us (97%)
  between operations  0.64 us (2%)
    pallas_call x1, Pallas kernels, on_device(): pl.pallas_call(functools.partial(window, n_gx, n_gy, nz), out_shape=(out,...  24 us
    pallas_call x1, Pallas kernels, on_device(): pl.pallas_call(hand_over, out_shape=(out, out), in_specs=[hbm, hbm], out_...  1.83 us

profile of v4, /device:TPU:0, one launch (start us, length us, event | category | flops | bytes accessed | tf_op | source)
XLA Modules:
  0.0 26.5 jit_solution(236625577869982181)
XLA Ops:
  0.6 24.0 %window.1 = (f32[64,8,128]{2,1,0:T(8,128)}, f32[64,8,128]{2,1,0:T(8,128)}) custom-call(s32[4]{0:T(128)} %holder_in.1, f32[4,12]{1,0:T(4,128)} %bitcast.8, bf16[32,16,128]{2,1,0:T(8,128)(2,1)} %bitcast.7, bf16[2,32]{1,0:T(2,128)(2,1)} %bitcast.9, s32[8,128]{1,0:T(8,128)} %classes_in.1, f32[64,8,128]{2,1,0:T(8,128)} %bitcast.6), custom_call_target="tpu_custom_call" | custom-call | tf_op jit(solution)/shard_map/window/pallas_call | solution.py:503
  24.7 1.8 %hand_over.1 = (f32[64,8,128]{2,1,0:T(8,128)}, f32[64,8,128]{2,1,0:T(8,128)}) custom-call(f32[64,8,128]{2,1,0:T(8,128)} %get-tuple-element.6.a, f32[64,8,128]{2,1,0:T(8,128)} %get-tuple-element.7.b), custom_call_target="tpu_custom_call" | custom-call | tf_op jit(solution)/shard_map/hand_over/pallas_call | solution.py:546

commit v5 on v4

--- a/solution.py
+++ b/solution.py
@@ -9,6 +9,7 @@
 
 MESH = pl.DeviceIdType.MESH
 COT, ST0, ST1, ADJ = range(4)
+PARTS = 4
 
 
 def window(
@@ -19,7 +20,7 @@
 ):
     gx, gy = lax.axis_index("gx"), lax.axis_index("gy")
     cx, cy = classes.shape
-    chips, hz = n_gy // 2, nz // 2
+    chips, hz, qz = n_gy // 2, nz // 2, nz // PARTS
     partner = gy + 1 - 2 * lax.rem(gy, 2)
     lane = lax.broadcasted_iota(jnp.int32, (cx, cy), 1)
     sub = lax.broadcasted_iota(jnp.int32, (cx, cy), 0)
@@ -98,11 +99,11 @@
         @pl.when(jnp.logical_not(y_has[side]))
         def _():
             for e in range(3):
-                for half in range(2):
+                for half in range(PARTS):
                     yr[e, half, side] = jnp.zeros((cx, cy), jnp.float32)
 
     def row_of(f, z):
-        return z + f * hz + lax.div(z, hz) * hz
+        return z + (f + lax.div(z, qz)) * qz
 
     for ref in (m0, m1, g0, g1):
         for q in range(ref.shape[0]):
@@ -162,7 +163,7 @@
 
     def x_copy(e, half, side):
         there = gx - 1 if side == 0 else gx + 1
-        part = pl.ds(0, 2 * nz + 4) if e == COT else pl.ds(half * nz, nz)
+        part = pl.ds(0, 2 * nz + 4) if e == COT else pl.ds(half * 2 * qz, 2 * qz)
         return pltpu.make_async_remote_copy(
             src_ref=xs.at[e, side, part], dst_ref=xr.at[e, 1 - side, part],
             send_sem=xsend.at[e, half, side], recv_sem=xrecv.at[e, half, 1 - side],
@@ -238,7 +239,7 @@
         return xr[e, 0, row], xr[e, 1, row]
 
     def field_near(e, f, z, value):
-        row, i, half = row_of(f, z), y_of[e], 0 if e == COT else lax.div(z, hz)
+        row, i, half = row_of(f, z), y_of[e], 0 if e == COT else lax.div(z, qz)
         return beside_x(value, *rows(e, row)) + beside_y(value, yr[i, half, 0], yr[i, half, 1], row)
 
     def keep_cot_near(z):
@@ -294,10 +295,10 @@
 
         return work
 
-    quarter = hz // 2
-    for half in range(2):
+    quarter = qz // 2
+    for half in range(PARTS):
         for f in range(2):
-            by_chunks(f * hz + half * quarter, quarter, 8, own_of(f), put_own, 0)
+            by_chunks(f * hz + half * quarter, quarter, 4, own_of(f), put_own, 0)
         start(ST0, half)
 
     before = pair_of(jnp.maximum(gy - 1, 0), jnp.where(gy > 0, 1.0, 0.0))
@@ -407,9 +408,9 @@
         m1[3, z + 1] = 0.75 + 0.5 * s
         return put_edges(ST1, m1, z, pair, carry)
 
-    for half in range(2):
+    for half in range(PARTS):
         arrived(ST0, half)
-        ys[1, half, 0], ys[1, half, 1] = by_chunks(half * hz, hz, 4, work1, put1, blank)
+        ys[1, half, 0], ys[1, half, 1] = by_chunks(half * qz, qz, 4, work1, put1, blank)
         start(ST1, half)
 
     def work2(z):
@@ -420,9 +421,9 @@
     def put2(z, pair, carry):
         return put_edges(ADJ, g1, z, pair, carry)
 
-    for half in range(2):
+    for half in range(PARTS):
         arrived(ST1, half)
-        ys[2, half, 0], ys[2, half, 1] = by_chunks(half * hz, hz, 4, work2, put2, blank)
+        ys[2, half, 0], ys[2, half, 1] = by_chunks(half * qz, qz, 4, work2, put2, blank)
         start(ADJ, half)
 
     def put_out(ref):
@@ -436,20 +437,20 @@
 
     def write(i, held, out, half):
         for f in range(2):
-            part = pl.ds(f * nz + half * hz, hz)
+            part = pl.ds(f * nz + half * qz, qz)
             copy = pltpu.make_async_copy(held.at[part], out.at[part], osem.at[i, half, f])
             copy.start()
             written.append(copy)
 
-    for half in range(2):
+    for half in range(PARTS):
         by_chunks(
-            half * hz, hz, 4, lambda z: forward(1, z, kept_near(near1, z)), put_out(held2), 0
+            half * qz, qz, 4, lambda z: forward(1, z, kept_near(near1, z)), put_out(held2), 0
         )
         write(0, held2, out2, half)
-    for half in range(2):
+    for half in range(PARTS):
         arrived(ADJ, half)
         by_chunks(
-            half * hz, hz, 4, lambda z: backward(0, z, kept_near(near0, z)), put_out(helds), 0
+            half * qz, qz, 4, lambda z: backward(0, z, kept_near(near0, z)), put_out(helds), 0
         )
         write(1, helds, outs, half)
 
@@ -458,7 +459,7 @@
             c.wait_send()
     each(COT, 0, lambda c: c.wait_send())
     for e in (ST0, ST1, ADJ):
-        for half in range(2):
+        for half in range(PARTS):
             each(e, half, lambda c: c.wait_send())
     for copy in written:
         copy.wait()
@@ -526,17 +527,17 @@
             pltpu.VMEM((layers, cx, cy), f32),
             pltpu.VMEM((4, 2, layers + 4, 1, cy), f32),
             pltpu.VMEM((4, 2, layers + 4, 1, cy), f32),
-            pltpu.VMEM((3, 2, 2, cx, cy), f32),
-            pltpu.VMEM((3, 2, 2, cx, cy), f32),
+            pltpu.VMEM((3, PARTS, 2, cx, cy), f32),
+            pltpu.VMEM((3, PARTS, 2, cx, cy), f32),
             pltpu.VMEM((5, 4, cx, cy), f32),
             dma((3, n_gy - 1)),
             dma((3, n_gy - 1)),
             dma((7,)),
-            dma((2, 2, 2)),
-            dma((4, 2, 2)),
-            dma((4, 2, 2)),
-            dma((3, 2, 2)),
-            dma((3, 2, 2)),
+            dma((2, PARTS, 2)),
+            dma((4, PARTS, 2)),
+            dma((4, PARTS, 2)),
+            dma((3, PARTS, 2)),
+            dma((3, PARTS, 2)),
         ],
         compiler_params=pltpu.CompilerParams(
             collective_id=0, has_side_effects=True, vmem_limit_bytes=60 * 1024 * 1024

time: 26.7 us -> 26.1 us (0.978)
  Pallas kernels: 25.8 us -> 25.3 us
    pallas_call x1, Pallas kernels: 24 us -> 23.5 us  [on_device(): pl.pallas_call(functools.partial(window, n_gx, n_gy, nz), out_shape=(out,...]
where the time goes in v5:
time: 26.1 us; the launch traced here: 25.9 us
  Pallas kernels  25.3 us (97%)
  between operations  0.64 us (2%)
    pallas_call x1, Pallas kernels, on_device(): pl.pallas_call(functools.partial(window, n_gx, n_gy, nz), out_shape=(out,...  23.5 us
    pallas_call x1, Pallas kernels, on_device(): pl.pallas_call(hand_over, out_shape=(out, out), in_specs=[hbm, hbm], out_...  1.83 us

profile of v5, /device:TPU:0, one launch (start us, length us, event | category | flops | bytes accessed | tf_op | source)
XLA Modules:
  0.0 25.9 jit_solution(1660166720090654439)
XLA Ops:
  0.6 23.5 %window.1 = (f32[64,8,128]{2,1,0:T(8,128)}, f32[64,8,128]{2,1,0:T(8,128)}) custom-call(s32[4]{0:T(128)} %holder_in.1, f32[4,12]{1,0:T(4,128)} %bitcast.8, bf16[32,16,128]{2,1,0:T(8,128)(2,1)} %bitcast.7, bf16[2,32]{1,0:T(2,128)(2,1)} %bitcast.9, s32[8,128]{1,0:T(8,128)} %classes_in.1, f32[64,8,128]{2,1,0:T(8,128)} %bitcast.6), custom_call_target="tpu_custom_call" | custom-call | tf_op jit(solution)/shard_map/window/pallas_call | solution.py:504
  24.1 1.8 %hand_over.1 = (f32[64,8,128]{2,1,0:T(8,128)}, f32[64,8,128]{2,1,0:T(8,128)}) custom-call(f32[64,8,128]{2,1,0:T(8,128)} %get-tuple-element.6.a, f32[64,8,128]{2,1,0:T(8,128)} %get-tuple-element.7.b), custom_call_target="tpu_custom_call" | custom-call | tf_op jit(solution)/shard_map/hand_over/pallas_call | solution.py:547
